TPU v7x, 32 devices: a whole 2x2x4 slice. The times are simulated.
32 devices in a mesh: hours: 2 (over x), row: 8 (over z, y), col: 2 (over core).
Axes of the slice: x: 2, y: 2, z: 4, core: 2. Of those that a mesh axis runs over, the one named last changes fastest.
Arguments:
- spectra: bfloat16 [24, 2, 64, 4096], P('hours', None, 'row', 'col'), parts along dimension 0, may hold values from -6 to 6
- masks: int32 [24, 64], P('hours', 'row'), parts along dimension 0, may hold values 0 or 1
Outputs:
- correlations: float32 [128, 2, 32, 128], P(('hours', 'row'), 'col'), parts along dimension 0
There are 2 independent parts, one for each index of `hours`. A program takes and returns all parts, laid end to end along the dimension named above; each array names one. Nothing has to cross between parts.
All inputs are finite; a program needn't handle non-finite values. No bound on the sum of `masks` on one device may be relied on, other than what follows from the above.
Results may differ from a plain program's by a relative error of at most 0.0054.
Values may be sent and summed in bfloat16 or wider, within the bound.
A program may use at most 128 MiB of HBM per device.

v0:
```python
import math

import jax
import jax.numpy as jnp
from jax import lax
from jax.sharding import PartitionSpec as P

F = 4096
SMOOTH = 32
LAGS = 128


EPSILON = 1e-05
BLOCK_LIMIT = 64


def with_halo(cells, sides, width):
    for axis, dim in sides:
        count = lax.axis_size(axis)
        ends = count - 1
        head = lax.slice_in_dim(cells, 0, width, axis=dim)
        tail = lax.slice_in_dim(cells, cells.shape[dim] - width, cells.shape[dim], axis=dim)
        cells = jnp.concatenate(
            [
                lax.ppermute(tail, axis, [(i, (i + 1) % count) for i in range(ends)]),
                cells,
                lax.ppermute(head, axis, [((i + 1) % count, i) for i in range(ends)]),
            ],
            axis=dim,
        )
    return cells


def cosine_table(first, count):
    freqs = first + jnp.arange(count, dtype=jnp.int32)
    shifts = jnp.arange(1, LAGS + 1, dtype=jnp.int32)
    phase = freqs[:, None] * shifts[None, :] % (2 * F)
    angle = jnp.pi * phase.astype(jnp.float32) / F
    factor = 1.0 / math.sqrt(F)
    return jnp.concatenate([jnp.cos(angle) * factor, -jnp.sin(angle) * factor], axis=0).astype(
        jnp.bfloat16
    )


def whiten(values, padded, live):
    total = lax.reduce_window(
        padded, jnp.array(0, padded.dtype), lax.add, (1, 1, 2 * SMOOTH + 1), (1, 1, 1), "VALID"
    )
    amplitude = total / (2 * SMOOTH + 1) + EPSILON
    return (values / amplitude[:, None] * live[:, None, :, None]).astype(jnp.bfloat16)


def stack_spectra(own, own_live, other, other_live):
    shape = (own.shape[2], other.shape[2], own.shape[3])
    real = jnp.zeros(shape, jnp.float32)
    imag = jnp.zeros(shape, jnp.float32)
    for window in range(own.shape[0]):
        left_re = own[window, 0].astype(jnp.float32)[:, None, :]
        left_im = own[window, 1].astype(jnp.float32)[:, None, :]
        right_re = other[window, 0].astype(jnp.float32)[None, :, :]
        right_im = other[window, 1].astype(jnp.float32)[None, :, :]
        real = real + (left_re * right_re + left_im * right_im)
        imag = imag + (left_im * right_re - left_re * right_im)
    count = jnp.maximum(jnp.dot(own_live.T, other_live, preferred_element_type=jnp.float32), 1.0)
    return (jnp.stack([real, imag], axis=2) / count[:, :, None, None]).astype(jnp.bfloat16)


def correlate(own, own_live, other, other_live, table):
    stacked = stack_spectra(own, own_live, other, other_live)
    rows = stacked.reshape(stacked.shape[0] * stacked.shape[1], -1)
    result = jnp.dot(rows, table, preferred_element_type=jnp.float32)
    return result.reshape(stacked.shape[0], stacked.shape[1], -1)


def magnitudes(values):
    return jnp.sqrt(values[:, 0] * values[:, 0] + values[:, 1] * values[:, 1])


def block_shards(total_shards, shard_rows):
    best = 1
    for factor in range(1, total_shards + 1):
        if total_shards % factor == 0 and factor * shard_rows <= BLOCK_LIMIT:
            best = factor
    return best


def fold_pairs(own, own_live, table, group, columns):

    def add_pieces(carry, piece, start):
        other, other_marks = piece
        shards = other.shape[2] // group
        per_block = block_shards(shards, group)
        width = per_block * group

        def one_block(number, total):
            first = number * width
            sub_spectra = lax.dynamic_slice_in_dim(other, first, width, 2)
            sub_live = lax.dynamic_slice_in_dim(other_marks, first, width, 2)[:, 0].astype(
                jnp.float32
            )
            block = correlate(own, own_live, sub_spectra, sub_live, table)
            block = block.reshape(
                block.shape[0], per_block, columns, group // columns, block.shape[2]
            )
            block = jnp.transpose(block, (0, 2, 1, 3, 4))
            block = block.reshape(block.shape[0], columns, width // columns, block.shape[4])
            slot = (start + first) // columns
            zero = jnp.zeros((), jnp.int32)
            return lax.dynamic_update_slice(
                total, block, (zero, zero, slot.astype(jnp.int32), zero)
            )

        return lax.fori_loop(0, shards // per_block, one_block, carry)

    return add_pieces


def per_device(spectra, masks):
    channels = spectra.shape[2]
    half_freq = spectra.shape[3]
    columns = lax.axis_size("col")
    column = lax.axis_index("col")
    partners = lax.axis_size("row") * channels
    live = masks.astype(jnp.float32)
    values = spectra.astype(jnp.float32)
    padded = with_halo(magnitudes(values), (("col", 2),), SMOOTH)
    whitened = whiten(values, padded, live)
    table = cosine_table(column * half_freq, half_freq)
    marks = live.astype(jnp.bfloat16)[:, None, :]
    adder = fold_pairs(whitened, live, table, channels, columns)
    empty = jnp.zeros((channels, columns, partners // columns, LAGS), jnp.float32)
    partial_sum = adder(
        empty,
        (
            lax.all_gather(whitened, "row", axis=2, tiled=True),
            lax.all_gather(marks, "row", axis=2, tiled=True),
        ),
        jnp.int32(0),
    )
    return lax.psum_scatter(partial_sum, "col", scatter_dimension=1, tiled=True)


def solution(mesh):
    placed = (P("hours", None, "row", "col"), P("hours", "row"))
    return jax.shard_map(
        per_device,
        mesh=mesh,
        in_specs=placed,
        out_specs=P(("hours", "row"), "col", None, None),
        check_vma=False,
    )
```

profile of v0, /device:TPU:0, one launch (start us, length us, event | category | flops | bytes accessed | tf_op | source)
XLA Modules:
  0.0 509.3 jit_solution(13442674106932536486)
XLA Ops:
  6.5 1.3 convert_element_type.552
  7.9 0.3 fusion.9
  8.2 2.4 collective-permute-start
  10.6 1.3 collective-permute-start.1
  12.0 1.7 collective-permute-done.1
  13.7 0.5 concatenate.7
  14.2 217.8 %reduce_window.7 = f32[12,8,2048]{2,1,0:T(8,128)S(1)} reduce-window(f32[12,8,2112]{2,1,0:T(8,128)S(1)} %concatenate.7, f32[]{:T(128)} %constant.50.clone.1), window={size=1x1x65}, to_apply=%region_0.0 | reduce-window | flops 12582912 | bytes 1597444 | tf_op jit(solution)/shard_map/reduce_window | solution.py:46
  232.1 1.2 multiply_convert_fusion
  233.3 27.7 %all-gather = bf16[12,64]{0,1:T(8,128)(2,1)S(1)} all-gather(bf16[12,8]{0,1:T(8,128)(2,1)S(1)} %get-tuple-element.81), channel_id=2, replica_groups=mesh['hours'=2,'row'=8,'col'=2] {'row'}, dimensions={1}, use_global_device_ids=true | all-gather | bytes 1728 | tf_op jit(solution)/shard_map/all_gather | solution.py:136
  261.0 0.1 convolution_maximum_fusion
  261.3 5.0 multiply_convert_fusion.2
  266.3 0.8 fusion.56
  267.2 1.2 fusion.57
  268.3 66.4 %all-gather.3.cloned.1.call-done = bf16[12,2,64,2048]{3,2,1,0:T(8,128)(2,1)} async-done(((bf16[12,2,8,2048]{3,2,1,0:T(8,128)(2,1)}), bf16[12,2,64,2048]{3,2,1,0:T(8,128)(2,1)}) %all-gather.3.cloned.1.call-update) | async-done | bytes 6291472 | tf_op jit(solution)/shard_map/all_gather | solution.py:135
  334.7 3.8 fusion.33
  338.5 1.6 fusion.32
  340.1 64.5 %add_add_fusion = f32[8,64,1,2048]{3,2,0,1:T(1,128)S(1)} fusion(f32[64,2048]{1,0:T(8,128)S(1)} %get-tuple-element.20, f32[8,2048]{1,0:T(8,128)S(1)} %get-tuple-element.54, f32[64,2048]{1,0:T(8,128)S(1)} %get-tuple-element.21, f32[8,2048]{1,0:T(8,128)S(1)} %get-tuple-element.55, f32[64,2048]{1,0:T(8,128)S(1)} %get-tuple-element.22, ...), kind=kLoop, calls=%fused_computation.3 | loop fusion | flops 49283072 | bytes 18350080 | tf_op jit(solution)/shard_map/while/body/eval_jaxpr/add | solution.py:62
  404.6 64.5 %subtract_add_fusion = f32[8,64,1,2048]{3,2,0,1:T(1,128)S(1)} fusion(f32[64,2048]{1,0:T(8,128)S(1)} %get-tuple-element.20, f32[8,2048]{1,0:T(8,128)S(1)} %get-tuple-element.54, f32[64,2048]{1,0:T(8,128)S(1)} %get-tuple-element.21, f32[8,2048]{1,0:T(8,128)S(1)} %get-tuple-element.55, f32[64,2048]{1,0:T(8,128)S(1)} %get-tuple-element.22, ...), kind=kLoop, calls=%fused_computation.2 | loop fusion | flops 49283072 | bytes 18350080 | tf_op jit(solution)/shard_map/while/body/eval_jaxpr/add | solution.py:63
  469.1 8.5 %pad_maximum_fusion = f32[8,64,2,2048]{3,2,0,1:T(2,128)} fusion(f32[8,64,1,2048]{3,2,0,1:T(1,128)S(1)} %subtract_add_fusion, f32[8,64,1,2048]{3,2,0,1:T(1,128)S(1)} %add_add_fusion), kind=kLoop, calls=%fused_computation | loop fusion | flops 2097152 | bytes 16777216 | tf_op jit(solution)/shard_map/while/body/eval_jaxpr/stack | solution.py:65
  477.6 11.8 %stack.11 = f32[8,8,2,4,4096]{4,0,3,2,1:T(8,128)} reshape(f32[8,64,2,2048]{3,2,0,1:T(2,128)} %pad_maximum_fusion) | data formatting | bytes 16777216 | tf_op jit(solution)/shard_map/while/body/eval_jaxpr/stack | solution.py:65
  489.4 4.7 fusion.1
  494.1 0.7 copy.8
  494.8 6.0 %reduce-scatter.2.cloned.1.call-done = f32[8,1,32,128]{3,0,2,1:T(8,128)} async-done(((f32[8,2,32,128]{3,0,2,1:T(8,128)}), f32[8,1,32,128]{3,0,2,1:T(8,128)}) %reduce-scatter.2.cloned.1.call-update) | async-done | bytes 131088 | tf_op jit(solution)/shard_map/reduce_scatter | solution.py:140
  500.9 1.6 copy.9
  (16 shorter events, 0.5 us)
Async XLA Ops:
  6.5 5.3 %copy-start.1 = (s32[12,8]{0,1:T(8,128)S(1)}, s32[12,8]{0,1:T(8,128)}, u32[]{:S(2)}) copy-start(s32[12,8]{0,1:T(8,128)} %param.3) | copy-start | bytes 1156
  6.5 328.2 %all-gather.3.cloned.1.call-start = ((), (), s32[]{:S(2)}) async-start(), calls=%async_computation.1 | async-start | bytes 7077888 | tf_op jit(solution)/shard_map/all_gather | solution.py:135
  7.9 224.2 %copy-start = (bf16[12,2,8,2048]{3,2,1,0:T(8,128)(2,1)S(1)}, bf16[12,2,8,2048]{3,2,1,0:T(8,128)(2,1)}, u32[]{:S(2)}) copy-start(bf16[12,2,8,2048]{3,2,1,0:T(8,128)(2,1)} %param.2) | copy-start | bytes 2359300
  8.2 3.8 collective-permute-start
  10.6 3.1 collective-permute-start.1
  233.3 267.6 %reduce-scatter.2.cloned.1.call-start = ((), (), s32[]{:S(2)}) async-start(), calls=%async_computation.2 | async-start | bytes 393216 | tf_op jit(solution)/shard_map/reduce_scatter | solution.py:140
Sparse Core Ops, SparseCore 0:
  233.4 101.2 all-gather.2
  495.0 5.8 reduce-scatter.1
where the time goes:
time: 510 us; the launch traced here: 509 us
  other arithmetic  371 us (73%)
  waiting for transfers between devices  74.2 us (15%)
  blocking collectives  27.7 us (5%)
  local copies, waits for them, and re-layouts  14.8 us (3%)
  between operations  13.6 us (3%)
    another operation x1, other arithmetic, whiten(): lax.reduce_window(padded, jnp.array(0, padded.dtype), lax.add, (1, 1, 2 *...  218 us
    all_gather x1, waiting for transfers between devices, per_device(): lax.all_gather(whitened, 'row', axis=2, tiled=True)  66.4 us
    add x1, other arithmetic, stack_spectra(): imag = imag + (left_im * right_re - left_re * right_im)  64.5 us
    add x1, other arithmetic, stack_spectra(): real = real + (left_re * right_re + left_im * right_im)  64.5 us
    all_gather x1, blocking collectives, per_device(): lax.all_gather(marks, 'row', axis=2, tiled=True)  27.7 us
    another operation x1, local copies, waits for them, and re-layouts, stack_spectra(): jnp.stack([real, imag], axis=2) / count[:, :, None, None]  11.8 us
  transfers between devices with their start and end apart: 4, of which 3 were waited for; matrix products, arithmetic and copies ran while one was open for 1% of the time, Pallas kernels for 0%

commit v1 on v0

v1 whole, which is shorter than its diff:
```python
import functools
import math

import jax
import jax.numpy as jnp
from jax import lax
from jax.experimental import pallas as pl
from jax.experimental.pallas import tpu as pltpu
from jax.sharding import PartitionSpec as P

F = 4096
SMOOTH = 32
LAGS = 128
EPSILON = 1e-05
LANES = 128
GROUP_SPLIT = 3
MESH = pl.DeviceIdType.MESH


def shifted(cells, by):
    return pltpu.roll(cells, (-by) % cells.shape[1], 1)


def kernel(
    rows, x_ref, m_ref, out_ref,
    mag, halo_out, halo_in, marks, live, sbuf, rbuf, re, im, su, di, table, part, mate, got,
    halo_sem, mark_send, mark_recv, a2a_send, a2a_recv, own_sem, mate_send, mate_recv, row_send, row_recv,
):
    windows, _, ch, half = x_ref.shape
    bins = half // rows
    hours, me, col = lax.axis_index("hours"), lax.axis_index("row"), lax.axis_index("col")
    other = 1 - col
    step_w = windows // GROUP_SPLIT

    def peer(k):
        return lax.rem(me + k, rows)

    def at_row(r):
        return (hours, r, col)

    at_mate = (hours, me, other)

    barrier = pltpu.get_barrier_semaphore()
    for k in range(1, rows):
        pl.semaphore_signal(barrier, inc=1, device_id=at_row(peer(k)), device_id_type=MESH)
    pl.semaphore_signal(barrier, inc=1, device_id=at_mate, device_id_type=MESH)

    def magnitude(a, b):
        return jnp.sqrt(a * a + b * b)

    def edges(w, _):
        a = x_ref[w, 0, :, half - LANES:].astype(jnp.float32)
        b = x_ref[w, 1, :, half - LANES:].astype(jnp.float32)
        c = x_ref[w, 0, :, :LANES].astype(jnp.float32)
        d = x_ref[w, 1, :, :LANES].astype(jnp.float32)
        first = col == 0
        halo_out[w] = magnitude(jnp.where(first, a, c), jnp.where(first, b, d))
        return 0

    lax.fori_loop(0, windows, edges, 0)

    lane = lax.broadcasted_iota(jnp.int32, (ch, LANES), 1)
    diag = lax.broadcasted_iota(jnp.int32, (ch, ch), 0) == lax.broadcasted_iota(jnp.int32, (ch, ch), 1)
    packed = jnp.zeros((ch, LANES), jnp.float32)
    for w in range(windows):
        row = m_ref[w:w + 1, :].astype(jnp.float32)
        column = jnp.sum(jnp.where(diag, row, 0.0), axis=1, keepdims=True)
        wide = jnp.broadcast_to(column, (ch, LANES))
        live[w] = wide
        packed = jnp.where(lane == w, wide, packed)
    marks[me] = packed

    pl.semaphore_wait(barrier, rows)

    halo = pltpu.make_async_remote_copy(
        src_ref=halo_out, dst_ref=halo_in, send_sem=halo_sem.at[0], recv_sem=halo_sem.at[1],
        device_id=at_mate, device_id_type=MESH,
    )
    halo.start()

    def mark_copy(k):
        return pltpu.make_async_remote_copy(
            src_ref=marks.at[me], dst_ref=marks.at[me], send_sem=mark_send.at[k], recv_sem=mark_recv.at[k],
            device_id=at_row(peer(k)), device_id_type=MESH,
        )

    for k in range(1, rows):
        mark_copy(k).start()

    def fill(w, _):
        a = x_ref[w, 0].astype(jnp.float32)
        b = x_ref[w, 1].astype(jnp.float32)
        mag[w, :, LANES:LANES + half] = magnitude(a, b)
        return 0

    lax.fori_loop(0, windows, fill, 0)
    halo.wait()

    def whiten(w, _):
        edge = halo_in[w]
        zero = jnp.zeros_like(edge)
        cells = jnp.concatenate(
            [jnp.where(col == 0, zero, edge), mag[w, :, LANES:LANES + half], jnp.where(col == 0, edge, zero)], axis=1
        )
        total = cells
        for by in (1, 2, 4, 8, 16):
            total = total + shifted(total, by)
        total = total + shifted(total, -SMOOTH) + shifted(cells, SMOOTH)
        total = total[:, LANES:LANES + half]
        amplitude = total / (2 * SMOOTH + 1) + EPSILON
        scale = live[w][:, :1] / amplitude
        both = jnp.concatenate(
            [x_ref[w, 0].astype(jnp.float32) * scale, x_ref[w, 1].astype(jnp.float32) * scale], axis=0
        ).astype(jnp.bfloat16)
        for r in range(rows):
            sbuf[r, w] = both[:, r * bins:(r + 1) * bins]
        return 0

    def share(g, k):
        span = pl.ds(g * step_w, step_w)
        return pltpu.make_async_remote_copy(
            src_ref=sbuf.at[peer(k), span], dst_ref=rbuf.at[me, span],
            send_sem=a2a_send.at[g, k], recv_sem=a2a_recv.at[g, k],
            device_id=at_row(peer(k)), device_id_type=MESH,
        )

    for g in range(GROUP_SPLIT):
        lax.fori_loop(g * step_w, (g + 1) * step_w, whiten, 0)
        for k in range(1, rows):
            share(g, k).start()

    own = pltpu.make_async_copy(sbuf.at[me], rbuf.at[me], own_sem)
    own.start()

    first = col * half + me * bins
    freq = first + lax.broadcasted_iota(jnp.int32, (bins, LAGS), 0)
    lag = 1 + lax.broadcasted_iota(jnp.int32, (bins, LAGS), 1)
    phase = freq * lag
    for p in range(2):
        turn = jnp.bitwise_and(phase + p * (F // 2), 2 * F - 1)
        wave = jnp.cos(turn.astype(jnp.float32) * (math.pi / F)) * (1.0 / math.sqrt(F))
        table[p * bins:(p + 1) * bins, :LAGS] = wave.astype(jnp.bfloat16)
        table[p * bins:(p + 1) * bins, LAGS:] = (wave if p == 0 else -wave).astype(jnp.bfloat16)

    own.wait()

    def widen(source):
        def one(w, _):
            both = rbuf[source, w].astype(jnp.float32)
            a, b = both[:ch], both[ch:]
            re[source, w] = a
            im[source, w] = b
            su[source, w] = a + b
            di[source, w] = a - b
            return 0

        lax.fori_loop(0, windows, one, 0)

    widen(me)
    for k in range(1, rows):
        mark_copy(k).wait_send()
        for g in range(GROUP_SPLIT):
            share(g, k).wait_send()

    def arrived(k, _):
        source = lax.rem(me + rows - k, rows)
        pltpu.make_async_remote_copy(
            src_ref=marks.at[source], dst_ref=marks.at[source], send_sem=mark_send.at[k], recv_sem=mark_recv.at[k],
            device_id=at_row(peer(k)), device_id_type=MESH,
        ).wait_recv()
        for g in range(GROUP_SPLIT):
            span = pl.ds(g * step_w, step_w)
            pltpu.make_async_remote_copy(
                src_ref=sbuf.at[source, span], dst_ref=rbuf.at[source, span],
                send_sem=a2a_send.at[g, k], recv_sem=a2a_recv.at[g, k],
                device_id=at_row(peer(k)), device_id_type=MESH,
            ).wait_recv()
        widen(source)
        return 0

    lax.fori_loop(1, rows, arrived, 0)

    quarter = ch // 2

    def pair(block_i, block_j):
        right = [(re[block_j, w], im[block_j, w], di[block_j, w]) for w in range(windows)]
        real, imag = [], []
        marks_j = marks[block_j]
        for i in range(ch):
            k1 = k2 = k3 = None
            for w in range(windows):
                c, d, e = right[w]
                a = re[block_i, w, i:i + 1, :]
                b = im[block_i, w, i:i + 1, :]
                s = su[block_i, w, i:i + 1, :]
                k1 = a * c if k1 is None else k1 + a * c
                k2 = b * d if k2 is None else k2 + b * d
                k3 = s * e if k3 is None else k3 + s * e
            count = jnp.sum(marks[block_i, i:i + 1, :] * marks_j, axis=1, keepdims=True)
            scale = 1.0 / jnp.maximum(count, 1.0)
            real.append((k1 + k2) * scale)
            imag.append((k3 - k1 + k2) * scale)
        left = jnp.concatenate(
            [jnp.concatenate(real, axis=0), jnp.concatenate(imag, axis=0)], axis=1
        ).astype(jnp.bfloat16)
        result = jnp.dot(left, table[...], preferred_element_type=jnp.float32)
        for i in range(ch):
            tile = result[i * ch:(i + 1) * ch]
            for h in range(2):
                part[h, block_i, i, block_j] = tile[h * quarter:(h + 1) * quarter, :LAGS]
            mirror = tile[:, LAGS:]
            for j in range(ch):
                part[i // quarter, block_j, j, block_i, i % quarter:i % quarter + 1, :] = mirror[j:j + 1, :]

    def owner(n):
        return lax.rem(me + 1 + n, rows)

    def to_mate(n):
        r = owner(n)
        return pltpu.make_async_remote_copy(
            src_ref=part.at[other, r], dst_ref=mate.at[r], send_sem=mate_send.at[n], recv_sem=mate_recv.at[n],
            device_id=at_mate, device_id_type=MESH,
        )

    def to_row(n):
        r = owner(n)
        return pltpu.make_async_remote_copy(
            src_ref=part.at[col, r], dst_ref=got.at[me], send_sem=row_send.at[n], recv_sem=row_recv.at[n],
            device_id=at_row(r), device_id_type=MESH,
        )

    def fold(n):
        to_mate(n).wait_recv()
        r = owner(n)
        for i in range(ch):
            part[col, r, i] = part[col, r, i] + mate[r, i]

    def sweep(n, _):
        def inner(m, _):
            pair(owner(n), owner(m))
            return 0

        lax.fori_loop(n, rows, inner, 0)
        to_mate(n).start()

        @pl.when(n > 0)
        def _():
            fold(n - 1)
            to_row(n - 1).start()

        return 0

    lax.fori_loop(0, rows, sweep, 0)
    fold(rows - 1)

    for i in range(ch):
        out_ref[i, 0] = part[col, me, i].reshape(rows * quarter, LAGS)

    def collect(n, _):
        source = lax.rem(me + rows + rows - 1 - n, rows)
        pltpu.make_async_remote_copy(
            src_ref=part.at[col, source], dst_ref=got.at[source], send_sem=row_send.at[n], recv_sem=row_recv.at[n],
            device_id=at_row(owner(n)), device_id_type=MESH,
        ).wait_recv()
        for i in range(ch):
            out_ref[i, 0] = out_ref[i, 0] + got[source, i].reshape(rows * quarter, LAGS)
        return 0

    lax.fori_loop(0, rows - 1, collect, 0)
    for n in range(rows):
        to_mate(n).wait_send()
        if n < rows - 1:
            to_row(n).wait_send()


def fused(spectra, masks):
    windows, _, ch, half = spectra.shape
    rows = lax.axis_size("row")
    bins = half // rows
    quarter = ch // 2
    f32, bf16 = jnp.float32, jnp.bfloat16
    dma = pltpu.SemaphoreType.DMA
    return pl.pallas_call(
        functools.partial(kernel, rows),
        out_shape=jax.ShapeDtypeStruct((ch, 1, rows * quarter, LAGS), f32),
        in_specs=[pl.BlockSpec(memory_space=pltpu.VMEM)] * 2,
        out_specs=pl.BlockSpec(memory_space=pltpu.VMEM),
        scratch_shapes=[
            pltpu.VMEM((windows, ch, half + 2 * LANES), f32),
            pltpu.VMEM((windows, ch, LANES), f32),
            pltpu.VMEM((windows, ch, LANES), f32),
            pltpu.VMEM((rows, ch, LANES), f32),
            pltpu.VMEM((windows, ch, LANES), f32),
            pltpu.VMEM((rows, windows, 2 * ch, bins), bf16),
            pltpu.VMEM((rows, windows, 2 * ch, bins), bf16),
            pltpu.VMEM((rows, windows, ch, bins), f32),
            pltpu.VMEM((rows, windows, ch, bins), f32),
            pltpu.VMEM((rows, windows, ch, bins), f32),
            pltpu.VMEM((rows, windows, ch, bins), f32),
            pltpu.VMEM((2 * bins, 2 * LAGS), bf16),
            pltpu.VMEM((2, rows, ch, rows, quarter, LAGS), f32),
            pltpu.VMEM((rows, ch, rows, quarter, LAGS), f32),
            pltpu.VMEM((rows, ch, rows, quarter, LAGS), f32),
            dma((2,)),
            dma((rows,)),
            dma((rows,)),
            dma((GROUP_SPLIT, rows)),
            dma((GROUP_SPLIT, rows)),
            dma,
            dma((rows,)),
            dma((rows,)),
            dma((rows,)),
            dma((rows,)),
        ],
        compiler_params=pltpu.CompilerParams(
            collective_id=0, has_side_effects=True, vmem_limit_bytes=48 * 1024 * 1024
        ),
    )(spectra, masks)


def with_halo(cells, width):
    head = cells[..., :width]
    tail = cells[..., cells.shape[-1] - width:]
    return jnp.concatenate(
        [lax.ppermute(tail, "col", [(0, 1)]), cells, lax.ppermute(head, "col", [(1, 0)])], axis=-1
    )


def cosine_table(first, count):
    freqs = first + jnp.arange(count, dtype=jnp.int32)
    shifts = jnp.arange(1, LAGS + 1, dtype=jnp.int32)
    phase = freqs[:, None] * shifts[None, :] % (2 * F)
    angle = jnp.pi * phase.astype(jnp.float32) / F
    factor = 1.0 / math.sqrt(F)
    return jnp.concatenate([jnp.cos(angle) * factor, -jnp.sin(angle) * factor], axis=0).astype(jnp.bfloat16)


def correlate(own, own_live, far, far_live, table):
    a, b = own[:, 0].astype(jnp.float32), own[:, 1].astype(jnp.float32)
    c, d = far[:, 0].astype(jnp.float32), far[:, 1].astype(jnp.float32)
    shape = (own.shape[2], far.shape[2], own.shape[3])
    real = jnp.zeros(shape, jnp.float32)
    imag = jnp.zeros(shape, jnp.float32)
    for w in range(own.shape[0]):
        real = real + (a[w, :, None] * c[w, None] + b[w, :, None] * d[w, None])
        imag = imag + (b[w, :, None] * c[w, None] - a[w, :, None] * d[w, None])
    count = jnp.maximum(jnp.dot(own_live.T, far_live, preferred_element_type=jnp.float32), 1.0)
    stacked = (jnp.stack([real, imag], axis=2) / count[:, :, None, None]).astype(jnp.bfloat16)
    lines = stacked.reshape(shape[0] * shape[1], -1)
    return jnp.dot(lines, table, preferred_element_type=jnp.float32).reshape(shape[0], shape[1], LAGS)


def ring(spectra, masks):
    ch, half = spectra.shape[2], spectra.shape[3]
    rows = lax.axis_size("row")
    me, col = lax.axis_index("row"), lax.axis_index("col")
    quarter = ch // 2
    live = masks.astype(jnp.float32)
    values = spectra.astype(jnp.float32)
    padded = with_halo(jnp.sqrt(values[:, 0] * values[:, 0] + values[:, 1] * values[:, 1]), SMOOTH)
    total = padded
    for by in (1, 2, 4, 8, 16, 32):
        total = total[..., :-by] + total[..., by:]
    total = total[..., :half] + padded[..., 2 * SMOOTH:]
    amplitude = total / (2 * SMOOTH + 1) + EPSILON
    whitened = (values / amplitude[:, None] * live[:, None, :, None]).astype(jnp.bfloat16)
    table = cosine_table(col * half, half)
    onward = [(r, (r + 1) % rows) for r in range(rows)]

    def step(n, carry):
        result, far, marks = carry
        block = correlate(whitened, live, far, marks.astype(jnp.float32), table)
        block = block.reshape(ch, 2, quarter, LAGS)
        source = lax.rem(me + rows - n, rows)
        result = lax.dynamic_update_slice(result, block, (0, 0, source * quarter, 0))
        return result, lax.ppermute(far, "row", onward), lax.ppermute(marks, "row", onward)

    empty = jnp.zeros((ch, 2, rows * quarter, LAGS), jnp.float32)
    result, _, _ = lax.fori_loop(0, rows, step, (empty, whitened, live.astype(jnp.bfloat16)))
    mine = lax.dynamic_slice_in_dim(result, col, 1, 1)
    other = lax.dynamic_slice_in_dim(result, 1 - col, 1, 1)
    return mine + lax.ppermute(other, "col", [(0, 1), (1, 0)])


def per_device(spectra, masks):
    windows, _, ch, half = spectra.shape
    rows = lax.axis_size("row")
    bins = half // rows
    fits = rows <= 8 and ch == 8 and bins % LANES == 0 and windows % GROUP_SPLIT == 0 and windows <= LANES
    return fused(spectra, masks) if fits else ring(spectra, masks)


def solution(mesh):
    return jax.shard_map(
        per_device,
        mesh=mesh,
        in_specs=(P("hours", None, "row", "col"), P("hours", "row")),
        out_specs=P(("hours", "row"), "col", None, None),
        check_vma=False,
    )
```

time: 510 us -> 61.8 us (0.12)
  the two profiles are of different devices: /device:TPU:0 before, /device:TPU:13 now
where the time goes in v1:
time: 61.8 us; the launch traced here: 61.6 us
  Pallas kernels  59 us (95%)
  local copies, waits for them, and re-layouts  2.56 us (4%)
    pallas_call x1, Pallas kernels, fused(): pl.pallas_call(functools.partial(kernel, rows), out_shape=jax.ShapeDtypeS...  59 us
    unnamed x4, local copies, waits for them, and re-layouts  2.56 us

profile of v1, /device:TPU:13, one launch (start us, length us, event | category | flops | bytes accessed | tf_op | source)
XLA Modules:
  0.0 61.6 jit_solution(17485265107336948670)
XLA Ops:
  0.0 0.8 %copy.3.m_ref = s32[12,8]{1,0:T(8,128)S(1)} copy(s32[12,8]{0,1:T(8,128)} %param.3) | data formatting | bytes 768 | tf_op args[1]
  0.8 0.0 copy-start
  0.8 1.1 %copy-done = bf16[12,2,8,2048]{3,2,1,0:T(8,128)(2,1)S(1)} copy-done((bf16[12,2,8,2048]{3,2,1,0:T(8,128)(2,1)S(1)}, bf16[12,2,8,2048]{3,2,1,0:T(8,128)(2,1)}, u32[]{:S(2)}) %copy-start) | copy-done | bytes 786456
  1.9 59.0 %shard_map.28 = f32[8,1,32,128]{3,2,1,0:T(8,128)S(1)} custom-call(bf16[12,2,8,2048]{3,2,1,0:T(8,128)(2,1)S(1)} %copy-done, s32[12,8]{1,0:T(8,128)S(1)} %copy.3.m_ref), custom_call_target="tpu_custom_call" | custom-call | tf_op jit(solution)/shard_map/pallas_call | solution.py:283
  60.9 0.7 %copy.5 = f32[8,1,32,128]{3,2,1,0:T(8,128)} copy(f32[8,1,32,128]{3,2,1,0:T(8,128)S(1)} %shard_map.28) | data formatting | bytes 262144
Async XLA Ops:
  0.8 1.1 %copy-start = (bf16[12,2,8,2048]{3,2,1,0:T(8,128)(2,1)S(1)}, bf16[12,2,8,2048]{3,2,1,0:T(8,128)(2,1)}, u32[]{:S(2)}) copy-start(bf16[12,2,8,2048]{3,2,1,0:T(8,128)(2,1)} %x_ref.1) | copy-start | bytes 2359300

commit v2 on v1

--- a/solution.py
+++ b/solution.py
@@ -23,11 +23,13 @@
 
 def kernel(
     rows, x_ref, m_ref, out_ref,
-    mag, halo_out, halo_in, marks, live, sbuf, rbuf, re, im, su, di, table, part, mate, got,
-    halo_sem, mark_send, mark_recv, a2a_send, a2a_recv, own_sem, mate_send, mate_recv, row_send, row_recv,
+    mag, halo_out, halo_in, marks, live, sbuf, rbuf, re, im, su, di, table, stash, part, mate, near, got,
+    halo_sem, mark_send, mark_recv, a2a_send, a2a_recv, own_sem, mate_send, mate_recv, near_send, near_recv, row_send, row_recv,
 ):
     windows, _, ch, half = x_ref.shape
     bins = half // rows
+    part_bins = bins // 2
+    pairs = rows // 2
     hours, me, col = lax.axis_index("hours"), lax.axis_index("row"), lax.axis_index("col")
     other = 1 - col
     step_w = windows // GROUP_SPLIT
@@ -113,14 +115,19 @@
             [x_ref[w, 0].astype(jnp.float32) * scale, x_ref[w, 1].astype(jnp.float32) * scale], axis=0
         ).astype(jnp.bfloat16)
         for r in range(rows):
-            sbuf[r, w] = both[:, r * bins:(r + 1) * bins]
+            for t in range(2):
+                start = r * bins + t * part_bins
+                sbuf[r, t, w] = both[:, start:start + part_bins]
         return 0
 
     def share(g, k):
-        span = pl.ds(g * step_w, step_w)
-        return pltpu.make_async_remote_copy(
-            src_ref=sbuf.at[peer(k), span], dst_ref=rbuf.at[me, span],
-            send_sem=a2a_send.at[g, k], recv_sem=a2a_recv.at[g, k],
+        if g < GROUP_SPLIT:
+            span = pl.ds(g * step_w, step_w)
+            source, target = sbuf.at[peer(k), 0, span], rbuf.at[me, 0, span]
+        else:
+            source, target = sbuf.at[peer(k), 1], rbuf.at[me, 1]
+        return pltpu.make_async_remote_copy(
+            src_ref=source, dst_ref=target, send_sem=a2a_send.at[g, k], recv_sem=a2a_recv.at[g, k],
             device_id=at_row(peer(k)), device_id_type=MESH,
         )
 
@@ -128,25 +135,28 @@
         lax.fori_loop(g * step_w, (g + 1) * step_w, whiten, 0)
         for k in range(1, rows):
             share(g, k).start()
+    for k in range(1, rows):
+        share(GROUP_SPLIT, k).start()
 
     own = pltpu.make_async_copy(sbuf.at[me], rbuf.at[me], own_sem)
     own.start()
 
-    first = col * half + me * bins
-    freq = first + lax.broadcasted_iota(jnp.int32, (bins, LAGS), 0)
-    lag = 1 + lax.broadcasted_iota(jnp.int32, (bins, LAGS), 1)
-    phase = freq * lag
-    for p in range(2):
-        turn = jnp.bitwise_and(phase + p * (F // 2), 2 * F - 1)
-        wave = jnp.cos(turn.astype(jnp.float32) * (math.pi / F)) * (1.0 / math.sqrt(F))
-        table[p * bins:(p + 1) * bins, :LAGS] = wave.astype(jnp.bfloat16)
-        table[p * bins:(p + 1) * bins, LAGS:] = (wave if p == 0 else -wave).astype(jnp.bfloat16)
+    for t in range(2):
+        first = col * half + me * bins + t * part_bins
+        freq = first + lax.broadcasted_iota(jnp.int32, (part_bins, LAGS), 0)
+        lag = 1 + lax.broadcasted_iota(jnp.int32, (part_bins, LAGS), 1)
+        phase = freq * lag
+        for p in range(2):
+            turn = jnp.bitwise_and(phase + p * (F // 2), 2 * F - 1)
+            wave = jnp.cos(turn.astype(jnp.float32) * (math.pi / F)) * (1.0 / math.sqrt(F))
+            table[t, p * part_bins:(p + 1) * part_bins, :LAGS] = wave.astype(jnp.bfloat16)
+            table[t, p * part_bins:(p + 1) * part_bins, LAGS:] = (wave if p == 0 else -wave).astype(jnp.bfloat16)
 
     own.wait()
 
-    def widen(source):
+    def widen(source, t):
         def one(w, _):
-            both = rbuf[source, w].astype(jnp.float32)
+            both = rbuf[source, t, w].astype(jnp.float32)
             a, b = both[:ch], both[ch:]
             re[source, w] = a
             im[source, w] = b
@@ -156,33 +166,37 @@
 
         lax.fori_loop(0, windows, one, 0)
 
-    widen(me)
-    for k in range(1, rows):
-        mark_copy(k).wait_send()
-        for g in range(GROUP_SPLIT):
-            share(g, k).wait_send()
-
-    def arrived(k, _):
+    def arrival(k, source, g):
+        if g < GROUP_SPLIT:
+            span = pl.ds(g * step_w, step_w)
+            target = rbuf.at[source, 0, span]
+        else:
+            target = rbuf.at[source, 1]
+        return pltpu.make_async_remote_copy(
+            src_ref=target, dst_ref=target, send_sem=a2a_send.at[g, k], recv_sem=a2a_recv.at[g, k],
+            device_id=at_row(peer(k)), device_id_type=MESH,
+        )
+
+    def first_half(k, _):
         source = lax.rem(me + rows - k, rows)
         pltpu.make_async_remote_copy(
             src_ref=marks.at[source], dst_ref=marks.at[source], send_sem=mark_send.at[k], recv_sem=mark_recv.at[k],
             device_id=at_row(peer(k)), device_id_type=MESH,
         ).wait_recv()
         for g in range(GROUP_SPLIT):
-            span = pl.ds(g * step_w, step_w)
-            pltpu.make_async_remote_copy(
-                src_ref=sbuf.at[source, span], dst_ref=rbuf.at[source, span],
-                send_sem=a2a_send.at[g, k], recv_sem=a2a_recv.at[g, k],
-                device_id=at_row(peer(k)), device_id_type=MESH,
-            ).wait_recv()
-        widen(source)
-        return 0
-
-    lax.fori_loop(1, rows, arrived, 0)
+            arrival(k, source, g).wait_recv()
+        widen(source, 0)
+        return 0
+
+    def second_half(k, _):
+        source = lax.rem(me + rows - k, rows)
+        arrival(k, source, GROUP_SPLIT).wait_recv()
+        widen(source, 1)
+        return 0
 
     quarter = ch // 2
 
-    def pair(block_i, block_j):
+    def stack(block_i, block_j):
         right = [(re[block_j, w], im[block_j, w], di[block_j, w]) for w in range(windows)]
         real, imag = [], []
         marks_j = marks[block_j]
@@ -200,10 +214,13 @@
             scale = 1.0 / jnp.maximum(count, 1.0)
             real.append((k1 + k2) * scale)
             imag.append((k3 - k1 + k2) * scale)
-        left = jnp.concatenate(
+        return jnp.concatenate(
             [jnp.concatenate(real, axis=0), jnp.concatenate(imag, axis=0)], axis=1
         ).astype(jnp.bfloat16)
-        result = jnp.dot(left, table[...], preferred_element_type=jnp.float32)
+
+    def pair(block_i, block_j, slot):
+        result = jnp.dot(stash[slot], table[0], preferred_element_type=jnp.float32)
+        result = result + jnp.dot(stack(block_i, block_j), table[1], preferred_element_type=jnp.float32)
         for i in range(ch):
             tile = result[i * ch:(i + 1) * ch]
             for h in range(2):
@@ -212,21 +229,17 @@
             for j in range(ch):
                 part[i // quarter, block_j, j, block_i, i % quarter:i % quarter + 1, :] = mirror[j:j + 1, :]
 
+    high, low = lax.div(me, 2), lax.rem(me, 2)
+
     def owner(n):
-        return lax.rem(me + 1 + n, rows)
+        place = lax.rem(high + 1 + lax.div(n, 2), pairs)
+        return 2 * place + lax.rem(low + 1 + lax.rem(n, 2), 2)
 
     def to_mate(n):
         r = owner(n)
         return pltpu.make_async_remote_copy(
             src_ref=part.at[other, r], dst_ref=mate.at[r], send_sem=mate_send.at[n], recv_sem=mate_recv.at[n],
             device_id=at_mate, device_id_type=MESH,
-        )
-
-    def to_row(n):
-        r = owner(n)
-        return pltpu.make_async_remote_copy(
-            src_ref=part.at[col, r], dst_ref=got.at[me], send_sem=row_send.at[n], recv_sem=row_recv.at[n],
-            device_id=at_row(r), device_id_type=MESH,
         )
 
     def fold(n):
@@ -235,9 +248,46 @@
         for i in range(ch):
             part[col, r, i] = part[col, r, i] + mate[r, i]
 
+    def to_near(q):
+        place = lax.rem(high + 1 + q, pairs)
+        return pltpu.make_async_remote_copy(
+            src_ref=part.at[col, owner(2 * q)], dst_ref=near.at[place],
+            send_sem=near_send.at[q], recv_sem=near_recv.at[q],
+            device_id=at_row(2 * high + 1 - low), device_id_type=MESH,
+        )
+
+    def to_row(q):
+        r = owner(2 * q + 1)
+        return pltpu.make_async_remote_copy(
+            src_ref=part.at[col, r], dst_ref=got.at[high], send_sem=row_send.at[q], recv_sem=row_recv.at[q],
+            device_id=at_row(r), device_id_type=MESH,
+        )
+
+    def join(q):
+        to_near(q).wait_recv()
+        r = owner(2 * q + 1)
+        place = lax.rem(high + 1 + q, pairs)
+        for i in range(ch):
+            part[col, r, i] = part[col, r, i] + near[place, i]
+
+    widen(me, 0)
+    lax.fori_loop(1, rows, first_half, 0)
+
+    def early(n, _):
+        def inner(m, _):
+            stash[n * rows + m] = stack(owner(n), owner(m))
+            return 0
+
+        lax.fori_loop(n, rows, inner, 0)
+        return 0
+
+    lax.fori_loop(0, rows, early, 0)
+    widen(me, 1)
+    lax.fori_loop(1, rows, second_half, 0)
+
     def sweep(n, _):
         def inner(m, _):
-            pair(owner(n), owner(m))
+            pair(owner(n), owner(m), n * rows + m)
             return 0
 
         lax.fori_loop(n, rows, inner, 0)
@@ -246,37 +296,53 @@
         @pl.when(n > 0)
         def _():
             fold(n - 1)
-            to_row(n - 1).start()
+
+        @pl.when(lax.rem(n, 2) == 1)
+        def _():
+            to_near(lax.div(n, 2)).start()
+
+        @pl.when(jnp.logical_and(n > 2, lax.rem(n, 2) == 1))
+        def _():
+            join(lax.div(n, 2) - 1)
+            to_row(lax.div(n, 2) - 1).start()
 
         return 0
 
     lax.fori_loop(0, rows, sweep, 0)
     fold(rows - 1)
+    join(pairs - 1)
 
     for i in range(ch):
         out_ref[i, 0] = part[col, me, i].reshape(rows * quarter, LAGS)
 
-    def collect(n, _):
-        source = lax.rem(me + rows + rows - 1 - n, rows)
+    def collect(q, _):
+        source = lax.rem(high + pairs + pairs - 1 - q, pairs)
         pltpu.make_async_remote_copy(
-            src_ref=part.at[col, source], dst_ref=got.at[source], send_sem=row_send.at[n], recv_sem=row_recv.at[n],
-            device_id=at_row(owner(n)), device_id_type=MESH,
+            src_ref=got.at[source], dst_ref=got.at[source], send_sem=row_send.at[q], recv_sem=row_recv.at[q],
+            device_id=at_row(owner(2 * q + 1)), device_id_type=MESH,
         ).wait_recv()
         for i in range(ch):
             out_ref[i, 0] = out_ref[i, 0] + got[source, i].reshape(rows * quarter, LAGS)
         return 0
 
-    lax.fori_loop(0, rows - 1, collect, 0)
+    lax.fori_loop(0, pairs - 1, collect, 0)
+    for k in range(1, rows):
+        mark_copy(k).wait_send()
+        for g in range(GROUP_SPLIT + 1):
+            share(g, k).wait_send()
     for n in range(rows):
         to_mate(n).wait_send()
-        if n < rows - 1:
-            to_row(n).wait_send()
+    for q in range(pairs):
+        to_near(q).wait_send()
+        if q < pairs - 1:
+            to_row(q).wait_send()
 
 
 def fused(spectra, masks):
     windows, _, ch, half = spectra.shape
     rows = lax.axis_size("row")
-    bins = half // rows
+    part_bins = half // rows // 2
+    pairs = rows // 2
     quarter = ch // 2
     f32, bf16 = jnp.float32, jnp.bfloat16
     dma = pltpu.SemaphoreType.DMA
@@ -291,26 +357,30 @@
             pltpu.VMEM((windows, ch, LANES), f32),
             pltpu.VMEM((rows, ch, LANES), f32),
             pltpu.VMEM((windows, ch, LANES), f32),
-            pltpu.VMEM((rows, windows, 2 * ch, bins), bf16),
-            pltpu.VMEM((rows, windows, 2 * ch, bins), bf16),
-            pltpu.VMEM((rows, windows, ch, bins), f32),
-            pltpu.VMEM((rows, windows, ch, bins), f32),
-            pltpu.VMEM((rows, windows, ch, bins), f32),
-            pltpu.VMEM((rows, windows, ch, bins), f32),
-            pltpu.VMEM((2 * bins, 2 * LAGS), bf16),
+            pltpu.VMEM((rows, 2, windows, 2 * ch, part_bins), bf16),
+            pltpu.VMEM((rows, 2, windows, 2 * ch, part_bins), bf16),
+            pltpu.VMEM((rows, windows, ch, part_bins), f32),
+            pltpu.VMEM((rows, windows, ch, part_bins), f32),
+            pltpu.VMEM((rows, windows, ch, part_bins), f32),
+            pltpu.VMEM((rows, windows, ch, part_bins), f32),
+            pltpu.VMEM((2, 2 * part_bins, 2 * LAGS), bf16),
+            pltpu.VMEM((rows * rows, ch * ch, 2 * part_bins), bf16),
             pltpu.VMEM((2, rows, ch, rows, quarter, LAGS), f32),
             pltpu.VMEM((rows, ch, rows, quarter, LAGS), f32),
-            pltpu.VMEM((rows, ch, rows, quarter, LAGS), f32),
+            pltpu.VMEM((pairs, ch, rows, quarter, LAGS), f32),
+            pltpu.VMEM((pairs, ch, rows, quarter, LAGS), f32),
             dma((2,)),
             dma((rows,)),
             dma((rows,)),
-            dma((GROUP_SPLIT, rows)),
-            dma((GROUP_SPLIT, rows)),
+            dma((GROUP_SPLIT + 1, rows)),
+            dma((GROUP_SPLIT + 1, rows)),
             dma,
             dma((rows,)),
             dma((rows,)),
-            dma((rows,)),
-            dma((rows,)),
+            dma((pairs,)),
+            dma((pairs,)),
+            dma((pairs,)),
+            dma((pairs,)),
         ],
         compiler_params=pltpu.CompilerParams(
             collective_id=0, has_side_effects=True, vmem_limit_bytes=48 * 1024 * 1024
@@ -386,7 +456,7 @@
     windows, _, ch, half = spectra.shape
     rows = lax.axis_size("row")
     bins = half // rows
-    fits = rows <= 8 and ch == 8 and bins % LANES == 0 and windows % GROUP_SPLIT == 0 and windows <= LANES
+    fits = rows in (2, 4, 6, 8) and ch == 8 and bins % (2 * LANES) == 0 and windows % GROUP_SPLIT == 0 and windows <= LANES
     return fused(spectra, masks) if fits else ring(spectra, masks)
 
 

time: 61.8 us -> 54.6 us (0.88)
  the two profiles are of different devices: /device:TPU:13 before, /device:TPU:0 now
where the time goes in v2:
time: 54.6 us; the launch traced here: 54.5 us
  Pallas kernels  51.9 us (95%)
  local copies, waits for them, and re-layouts  2.56 us (5%)
    pallas_call x1, Pallas kernels, fused(): pl.pallas_call(functools.partial(kernel, rows), out_shape=jax.ShapeDtypeS...  51.9 us
    unnamed x4, local copies, waits for them, and re-layouts  2.56 us

profile of v2, /device:TPU:0, one launch (start us, length us, event | category | flops | bytes accessed | tf_op | source)
XLA Modules:
  0.0 54.5 jit_solution(15067125571210311486)
XLA Ops:
  0.0 0.8 %copy.3.m_ref = s32[12,8]{1,0:T(8,128)S(1)} copy(s32[12,8]{0,1:T(8,128)} %param.3) | data formatting | bytes 768 | tf_op args[1]
  0.8 0.0 copy-start
  0.8 1.1 %copy-done = bf16[12,2,8,2048]{3,2,1,0:T(8,128)(2,1)S(1)} copy-done((bf16[12,2,8,2048]{3,2,1,0:T(8,128)(2,1)S(1)}, bf16[12,2,8,2048]{3,2,1,0:T(8,128)(2,1)}, u32[]{:S(2)}) %copy-start) | copy-done | bytes 786456
  1.9 51.9 %shard_map.28 = f32[8,1,32,128]{3,2,1,0:T(8,128)S(1)} custom-call(bf16[12,2,8,2048]{3,2,1,0:T(8,128)(2,1)S(1)} %copy-done, s32[12,8]{1,0:T(8,128)S(1)} %copy.3.m_ref), custom_call_target="tpu_custom_call" | custom-call | tf_op jit(solution)/shard_map/pallas_call | solution.py:349
  53.8 0.7 %copy.5 = f32[8,1,32,128]{3,2,1,0:T(8,128)} copy(f32[8,1,32,128]{3,2,1,0:T(8,128)S(1)} %shard_map.28) | data formatting | bytes 262144
Async XLA Ops:
  0.8 1.1 %copy-start = (bf16[12,2,8,2048]{3,2,1,0:T(8,128)(2,1)S(1)}, bf16[12,2,8,2048]{3,2,1,0:T(8,128)(2,1)}, u32[]{:S(2)}) copy-start(bf16[12,2,8,2048]{3,2,1,0:T(8,128)(2,1)} %x_ref.1) | copy-start | bytes 2359300

commit v3 on v2

--- a/solution.py
+++ b/solution.py
@@ -13,7 +13,7 @@
 LAGS = 128
 EPSILON = 1e-05
 LANES = 128
-GROUP_SPLIT = 3
+GROUP_SPLIT = 6
 MESH = pl.DeviceIdType.MESH
 
 
@@ -72,6 +72,13 @@
         packed = jnp.where(lane == w, wide, packed)
     marks[me] = packed
 
+    def fill(w, _):
+        a = x_ref[w, 0].astype(jnp.float32)
+        b = x_ref[w, 1].astype(jnp.float32)
+        mag[w, :, LANES:LANES + half] = magnitude(a, b)
+        return 0
+
+    lax.fori_loop(0, windows, fill, 0)
     pl.semaphore_wait(barrier, rows)
 
     halo = pltpu.make_async_remote_copy(
@@ -89,13 +96,6 @@
     for k in range(1, rows):
         mark_copy(k).start()
 
-    def fill(w, _):
-        a = x_ref[w, 0].astype(jnp.float32)
-        b = x_ref[w, 1].astype(jnp.float32)
-        mag[w, :, LANES:LANES + half] = magnitude(a, b)
-        return 0
-
-    lax.fori_loop(0, windows, fill, 0)
     halo.wait()
 
     def whiten(w, _):
@@ -131,11 +131,12 @@
             device_id=at_row(peer(k)), device_id_type=MESH,
         )
 
+    order = sorted(range(1, rows), key=lambda k: abs(2 * k - rows))
     for g in range(GROUP_SPLIT):
         lax.fori_loop(g * step_w, (g + 1) * step_w, whiten, 0)
-        for k in range(1, rows):
+        for k in order:
             share(g, k).start()
-    for k in range(1, rows):
+    for k in order:
         share(GROUP_SPLIT, k).start()
 
     own = pltpu.make_async_copy(sbuf.at[me], rbuf.at[me], own_sem)

time: 54.6 us -> 53.5 us (0.980)
  Pallas kernels: 51.9 us -> 50.8 us
    pallas_call x1, Pallas kernels: 51.9 us -> 50.8 us  [fused(): pl.pallas_call(functools.partial(kernel, rows), out_shape=jax.ShapeDtypeS...]
where the time goes in v3:
time: 53.5 us; the launch traced here: 53.3 us
  Pallas kernels  50.8 us (95%)
  local copies, waits for them, and re-layouts  2.56 us (5%)
    pallas_call x1, Pallas kernels, fused(): pl.pallas_call(functools.partial(kernel, rows), out_shape=jax.ShapeDtypeS...  50.8 us
    unnamed x4, local copies, waits for them, and re-layouts  2.56 us

profile of v3, /device:TPU:0, one launch (start us, length us, event | category | flops | bytes accessed | tf_op | source)
XLA Modules:
  0.0 53.3 jit_solution(4995399711091890945)
XLA Ops:
  0.0 0.8 %copy.3.m_ref = s32[12,8]{1,0:T(8,128)S(1)} copy(s32[12,8]{0,1:T(8,128)} %param.3) | data formatting | bytes 768 | tf_op args[1]
  0.8 0.0 copy-start
  0.8 1.1 %copy-done = bf16[12,2,8,2048]{3,2,1,0:T(8,128)(2,1)S(1)} copy-done((bf16[12,2,8,2048]{3,2,1,0:T(8,128)(2,1)S(1)}, bf16[12,2,8,2048]{3,2,1,0:T(8,128)(2,1)}, u32[]{:S(2)}) %copy-start) | copy-done | bytes 786456
  1.9 50.8 %shard_map.28 = f32[8,1,32,128]{3,2,1,0:T(8,128)S(1)} custom-call(bf16[12,2,8,2048]{3,2,1,0:T(8,128)(2,1)S(1)} %copy-done, s32[12,8]{1,0:T(8,128)S(1)} %copy.3.m_ref), custom_call_target="tpu_custom_call" | custom-call | tf_op jit(solution)/shard_map/pallas_call | solution.py:350
  52.7 0.7 %copy.5 = f32[8,1,32,128]{3,2,1,0:T(8,128)} copy(f32[8,1,32,128]{3,2,1,0:T(8,128)S(1)} %shard_map.28) | data formatting | bytes 262144
Async XLA Ops:
  0.8 1.1 %copy-start = (bf16[12,2,8,2048]{3,2,1,0:T(8,128)(2,1)S(1)}, bf16[12,2,8,2048]{3,2,1,0:T(8,128)(2,1)}, u32[]{:S(2)}) copy-start(bf16[12,2,8,2048]{3,2,1,0:T(8,128)(2,1)} %x_ref.1) | copy-start | bytes 2359300

commit v4 on v3

--- a/solution.py
+++ b/solution.py
@@ -59,7 +59,7 @@
         halo_out[w] = magnitude(jnp.where(first, a, c), jnp.where(first, b, d))
         return 0
 
-    lax.fori_loop(0, windows, edges, 0)
+    lax.fori_loop(0, windows, edges, 0, unroll=4)
 
     lane = lax.broadcasted_iota(jnp.int32, (ch, LANES), 1)
     diag = lax.broadcasted_iota(jnp.int32, (ch, ch), 0) == lax.broadcasted_iota(jnp.int32, (ch, ch), 1)
@@ -78,7 +78,7 @@
         mag[w, :, LANES:LANES + half] = magnitude(a, b)
         return 0
 
-    lax.fori_loop(0, windows, fill, 0)
+    lax.fori_loop(0, windows, fill, 0, unroll=2)
     pl.semaphore_wait(barrier, rows)
 
     halo = pltpu.make_async_remote_copy(
@@ -133,7 +133,7 @@
 
     order = sorted(range(1, rows), key=lambda k: abs(2 * k - rows))
     for g in range(GROUP_SPLIT):
-        lax.fori_loop(g * step_w, (g + 1) * step_w, whiten, 0)
+        lax.fori_loop(g * step_w, (g + 1) * step_w, whiten, 0, unroll=True)
         for k in order:
             share(g, k).start()
     for k in order:
@@ -165,7 +165,7 @@
             di[source, w] = a - b
             return 0
 
-        lax.fori_loop(0, windows, one, 0)
+        lax.fori_loop(0, windows, one, 0, unroll=True)
 
     def arrival(k, source, g):
         if g < GROUP_SPLIT:

time: 53.5 us -> 52.5 us (0.981)
  Pallas kernels: 50.8 us -> 49.8 us
    pallas_call x1, Pallas kernels: 50.8 us -> 49.8 us  [fused(): pl.pallas_call(functools.partial(kernel, rows), out_shape=jax.ShapeDtypeS...]
where the time goes in v4:
time: 52.5 us; the launch traced here: 52.3 us
  Pallas kernels  49.8 us (95%)
  local copies, waits for them, and re-layouts  2.56 us (5%)
    pallas_call x1, Pallas kernels, fused(): pl.pallas_call(functools.partial(kernel, rows), out_shape=jax.ShapeDtypeS...  49.8 us
    unnamed x4, local copies, waits for them, and re-layouts  2.56 us

profile of v4, /device:TPU:0, one launch (start us, length us, event | category | flops | bytes accessed | tf_op | source)
XLA Modules:
  0.0 52.3 jit_solution(14773699089533759174)
XLA Ops:
  0.0 0.8 %copy.3.m_ref = s32[12,8]{1,0:T(8,128)S(1)} copy(s32[12,8]{0,1:T(8,128)} %param.3) | data formatting | bytes 768 | tf_op args[1]
  0.8 0.0 copy-start
  0.8 1.1 %copy-done = bf16[12,2,8,2048]{3,2,1,0:T(8,128)(2,1)S(1)} copy-done((bf16[12,2,8,2048]{3,2,1,0:T(8,128)(2,1)S(1)}, bf16[12,2,8,2048]{3,2,1,0:T(8,128)(2,1)}, u32[]{:S(2)}) %copy-start) | copy-done | bytes 786456
  1.9 49.8 %shard_map.28 = f32[8,1,32,128]{3,2,1,0:T(8,128)S(1)} custom-call(bf16[12,2,8,2048]{3,2,1,0:T(8,128)(2,1)S(1)} %copy-done, s32[12,8]{1,0:T(8,128)S(1)} %copy.3.m_ref), custom_call_target="tpu_custom_call" | custom-call | tf_op jit(solution)/shard_map/pallas_call | solution.py:350
  51.7 0.7 %copy.5 = f32[8,1,32,128]{3,2,1,0:T(8,128)} copy(f32[8,1,32,128]{3,2,1,0:T(8,128)S(1)} %shard_map.28) | data formatting | bytes 262144
Async XLA Ops:
  0.8 1.1 %copy-start = (bf16[12,2,8,2048]{3,2,1,0:T(8,128)(2,1)S(1)}, bf16[12,2,8,2048]{3,2,1,0:T(8,128)(2,1)}, u32[]{:S(2)}) copy-start(bf16[12,2,8,2048]{3,2,1,0:T(8,128)(2,1)} %x_ref.1) | copy-start | bytes 2359300
